TPU v7x, 32 devices: a whole 2x2x4 slice. The times are simulated.
32 devices in a mesh: left: 8 (over y, x, core), right: 4 (over z).
Axes of the slice: x: 2, y: 2, z: 4, core: 2. Of those that a mesh axis runs over, the one named last changes fastest.
Arguments:
- corner: bfloat16 [32, 256, 256], P(('left', 'right')), may hold values from -6 to 6
- edge_row: bfloat16 [64, 32, 256, 256], P('left', 'right'), may hold values from -0.0625 to 0.0625
- source_row: int32 [64, 32], P('left', 'right'), may hold values from 0 to 31, as said below
- proj_row: bfloat16 [64, 256, 256], P('left'), may hold values from -0.375 to 0.375
- edge_col: bfloat16 [16, 80, 256, 256], P('right', 'left'), may hold values from -0.0390625 to 0.0390625
- source_col: int32 [16, 80], P('right', 'left'), may hold values from 0 to 63, as said below
- proj_col: bfloat16 [16, 256, 256], P('right'), may hold values from -0.375 to 0.375
Outputs:
- absorbed_row: bfloat16 [64, 256, 256], P(('left', 'right'))
- new_corner: bfloat16 [16, 256, 256], P('right', 'left')
Inputs may be any that keep to these rules, and one draw needn't show every extreme that they name: source_row[f, j] is a sector whose block lies on a device with right index j // 8, that is (source_row[f, j]) % 4 == j // 8. source_col[g, j] is a sector of the left index j // 10: source_col[g, j] // 8 == j // 10.
All inputs are finite; a program needn't handle non-finite values.
Results may differ from a plain program's by a relative error of at most 0.03.
Values may be sent and summed in bfloat16 or wider, within the bound.
A program may use at most 128 MiB of HBM per device.

v0:
```python
import jax
import jax.numpy as jnp
from jax import lax
from jax.sharding import PartitionSpec as P


def body(corner, edge_row, source_row, proj_row, edge_col, source_col, proj_col):
    right_count = lax.axis_size("right")
    held_count = corner.shape[0]
    gathered = lax.all_gather(corner, "left", axis=0, tiled=True)
    block_span = held_count * right_count
    local_index = source_row // block_span * held_count + source_row % held_count
    picked = jnp.take(gathered, local_index, axis=0)
    partial_value = jnp.einsum(
        "fkab,fkbc->fac", picked, edge_row, preferred_element_type=jnp.float32
    )
    rows_here = partial_value.shape[0] // right_count
    summed = lax.psum_scatter(
        partial_value.astype(jnp.bfloat16), "right", scatter_dimension=0, tiled=True
    )
    start_row = lax.axis_index("right") * rows_here
    proj_mine = lax.dynamic_slice_in_dim(proj_row, start_row, rows_here, 0)
    absorbed = jnp.einsum(
        "fba,fbc->fac", proj_mine, summed, preferred_element_type=jnp.float32
    ).astype(jnp.bfloat16)
    row_whole = lax.all_gather(absorbed, "right", axis=0, tiled=True)
    row_base = lax.axis_index("left") * row_whole.shape[0]
    picked_col = jnp.take(row_whole, source_col - row_base, axis=0)
    partial_col = jnp.einsum(
        "gkab,gkbc->gac", edge_col, picked_col, preferred_element_type=jnp.float32
    )
    col_sum = lax.psum_scatter(
        partial_col.astype(jnp.bfloat16), "left", scatter_dimension=1, tiled=True
    )
    new_corner = jnp.einsum(
        "gab,gbc->gac", col_sum, proj_col, preferred_element_type=jnp.float32
    ).astype(jnp.bfloat16)
    return (absorbed, new_corner)


def solution(mesh):
    in_specs = (
        P(("left", "right"), None, None),
        P("left", "right", None, None),
        P("left", "right"),
        P("left", None, None),
        P("right", "left", None, None),
        P("right", "left"),
        P("right", None, None),
    )
    out_specs = (P(("left", "right"), None, None), P("right", "left", None))
    return jax.shard_map(body, mesh=mesh, in_specs=in_specs, out_specs=out_specs, check_vma=False)
```

profile of v0, /device:TPU:0, one launch (start us, length us, event | category | flops | bytes accessed | tf_op | source)
XLA Modules:
  0.0 162.6 jit_solution(234019364434056516)
XLA Ops:
  7.2 0.0 copy-start
  7.2 0.0 all-gather.3.cloned.1.call-start
  7.2 0.7 all-gather.3.cloned.1.call-update
  7.9 0.0 reduce-scatter.3.cloned.1.call-start
  8.0 0.7 compare_and_fusion
  8.7 0.1 reshape.16
  8.7 27.4 %all-gather.3.cloned.1.call-done = bf16[8,256,256]{2,1,0:T(8,128)(2,1)} async-done(((bf16[1,256,256]{2,1,0:T(8,128)(2,1)}), bf16[8,256,256]{2,1,0:T(8,128)(2,1)}) %all-gather.3.cloned.1.call-update) | async-done | bytes 1048592 | tf_op jit(solution)/shard_map/all_gather | solution.py:10
  36.1 6.7 %gather_fusion = bf16[64,256,256]{2,1,0:T(8,128)(2,1)} fusion(bf16[8,256,256]{2,1,0:T(8,128)(2,1)} %all-gather.3.cloned.1.call-done, s32[1024]{0:T(1024)S(1)} %pad_clamp_fusion.1), kind=kCustom, calls=%fused_computation | custom fusion | bytes 16777472 | tf_op jit(solution)/shard_map/jit(_take)/gather | solution.py:13
  42.9 0.0 copy-start.2
  42.9 9.2 %bitcast_convert_fusion = bf16[8,256,256]{2,1,0:T(8,128)(2,1)} fusion(bf16[8,8,256,256]{3,2,1,0:T(8,128)(2,1)} %param.8, bf16[8,8,256,256]{3,2,1,0:T(8,128)(2,1)} %bitcast.19, pred[8,8]{1,0:T(8,128)(4,1)S(1)} %get-tuple-element.4), kind=kOutput, calls=%fused_computation.10 | convolution fusion | flops 2152202240 | bytes 17825856 | tf_op jit(solution)/shard_map/fkab,fkbc->fac/dot_general | solution.py:14
  52.1 0.0 reduce-scatter.3.cloned.1.call-update
  52.1 0.0 all-gather.5.cloned.1.call-start
  52.2 27.2 %reduce-scatter.3.cloned.1.call-done = bf16[2,256,256]{2,1,0:T(8,128)(2,1)} async-done(((bf16[8,256,256]{2,1,0:T(8,128)(2,1)}), bf16[2,256,256]{2,1,0:T(8,128)(2,1)}) %reduce-scatter.3.cloned.1.call-update) | async-done | bytes 262160 | tf_op jit(solution)/shard_map/reduce_scatter | solution.py:18
  79.4 0.0 copy-done
  79.4 1.9 %convolution_convert_fusion = bf16[2,256,256]{2,1,0:T(8,128)(2,1)} fusion(bf16[2,256,256]{2,1,0:T(8,128)(2,1)} %reduce-scatter.3.cloned.1.call-done, bf16[8,256,256]{2,1,0:T(8,128)(2,1)S(1)} %copy-done, s32[]{:T(128)S(6)} %select_n.30), kind=kOutput, calls=%fused_computation.14 | convolution fusion | flops 67239936 | bytes 786436 | tf_op jit(solution)/shard_map/fba,fbc->fac/dot_general | solution.py:23
  81.4 0.0 all-gather.5.cloned.1.call-update
  81.4 0.0 reduce-scatter.5.cloned.1.call-start
  81.4 0.0 copy-done.2
  81.5 0.1 reshape.24
  81.6 26.7 %all-gather.5.cloned.1.call-done = bf16[8,256,256]{2,1,0:T(8,128)(2,1)} async-done(((bf16[2,256,256]{2,1,0:T(8,128)(2,1)}), bf16[8,256,256]{2,1,0:T(8,128)(2,1)}) %all-gather.5.cloned.1.call-update) | async-done | bytes 1048592 | tf_op jit(solution)/shard_map/all_gather | solution.py:26
  108.3 5.8 %gather_fusion.1 = bf16[40,256,256]{2,1,0:T(8,128)(2,1)} fusion(bf16[8,256,256]{2,1,0:T(8,128)(2,1)} %all-gather.5.cloned.1.call-done, s32[1024]{0:T(1024)S(1)} %pad_clamp_fusion), kind=kCustom, calls=%fused_computation.1 | custom fusion | bytes 10485920 | tf_op jit(solution)/shard_map/jit(_take)/gather | solution.py:28
  114.1 0.0 copy-start.1
  114.1 6.5 %fusion.16 = bf16[4,256,256]{2,1,0:T(8,128)(2,1)} fusion(bf16[4,10,256,256]{3,2,1,0:T(8,128)(2,1)} %param.11, bf16[4,10,256,256]{3,2,1,0:T(8,128)(2,1)} %bitcast.20, pred[4,10]{1,0:T(4,128)(4,1)S(1)} %get-tuple-element.2), kind=kOutput, calls=%fused_computation.13 | convolution fusion | flops 1345060864 | bytes 11010088 | tf_op jit(solution)/shard_map/gkab,gkbc->gac/dot_general | solution.py:29
  120.6 0.0 reduce-scatter.5.cloned.1.call-update
  120.6 33.7 %reduce-scatter.5.cloned.1.call-done = bf16[4,32,256]{2,1,0:T(8,128)(2,1)} async-done(((bf16[4,256,256]{2,1,0:T(8,128)(2,1)}), bf16[4,32,256]{2,1,0:T(8,128)(2,1)}) %reduce-scatter.5.cloned.1.call-update) | async-done | bytes 65552 | tf_op jit(solution)/shard_map/reduce_scatter | solution.py:32
  154.4 0.0 copy-done.1
  154.4 1.7 %convolution_convert_fusion.1 = bf16[4,32,256]{2,1,0:T(8,128)(2,1)} fusion(bf16[4,32,256]{2,1,0:T(8,128)(2,1)} %reduce-scatter.5.cloned.1.call-done, bf16[4,256,256]{2,1,0:T(8,128)(2,1)S(1)} %copy-done.1), kind=kOutput, calls=%fused_computation.15 | convolution fusion | flops 16809984 | bytes 655360 | tf_op jit(solution)/shard_map/gab,gbc->gac/dot_general | solution.py:35
  (3 shorter events, 0.0 us)
Async XLA Ops:
  7.2 72.3 %copy-start = (bf16[8,256,256]{2,1,0:T(8,128)(2,1)S(1)}, bf16[8,256,256]{2,1,0:T(8,128)(2,1)}, u32[]{:S(2)}) copy-start(bf16[8,256,256]{2,1,0:T(8,128)(2,1)} %param.10) | copy-start | bytes 3145732
  7.2 28.9 %all-gather.3.cloned.1.call-start = ((), (), s32[]{:S(2)}) async-start(), calls=%async_computation.2 | async-start | bytes 1179648 | tf_op jit(solution)/shard_map/all_gather | solution.py:10
  7.9 71.5 %reduce-scatter.3.cloned.1.call-start = ((), (), s32[]{:S(2)}) async-start(), calls=%async_computation.3 | async-start | bytes 1310720 | tf_op jit(solution)/shard_map/reduce_scatter | solution.py:18
  42.9 38.6 %copy-start.2 = (s32[4,10]{1,0:T(4,128)S(1)}, s32[4,10]{1,0:T(4,128)}, u32[]{:S(2)}) copy-start(s32[4,10]{1,0:T(4,128)} %param.12) | copy-start | bytes 484
  52.1 56.1 %all-gather.5.cloned.1.call-start = ((), (), s32[]{:S(2)}) async-start(), calls=%async_computation.4 | async-start | bytes 1310720 | tf_op jit(solution)/shard_map/all_gather | solution.py:26
  81.4 73.0 %reduce-scatter.5.cloned.1.call-start = ((), (), s32[]{:S(2)}) async-start(), calls=%async_computation.5 | async-start | bytes 589824 | tf_op jit(solution)/shard_map/reduce_scatter | solution.py:32
  114.1 40.3 %copy-start.1 = (bf16[4,256,256]{2,1,0:T(8,128)(2,1)S(1)}, bf16[4,256,256]{2,1,0:T(8,128)(2,1)}, u32[]{:S(2)}) copy-start(bf16[4,256,256]{2,1,0:T(8,128)(2,1)} %param.13) | copy-start | bytes 1572868
Sparse Core Ops, SparseCore 0:
  9.9 26.1 all-gather.2
  52.2 27.1 reduce-scatter.2
  81.7 26.5 all-gather.4
  120.8 33.5 reduce-scatter.4
where the time goes:
time: 163 us
  waiting for transfers between devices  116 us (71%)
  matrix products  19.4 us (12%)
  between operations  13.8 us (8%)
  local copies, waits for them, and re-layouts  12.7 us (8%)
    reduce_scatter x1, waiting for transfers between devices, body(): lax.psum_scatter(partial_col.astype(jnp.bfloat16), 'left', scatter_dimens...  33.7 us
    all_gather x1, waiting for transfers between devices, body(): gathered = lax.all_gather(corner, 'left', axis=0, tiled=True)  27.4 us
    reduce_scatter x1, waiting for transfers between devices, body(): lax.psum_scatter(partial_value.astype(jnp.bfloat16), 'right', scatter_dim...  27.2 us
    all_gather x1, waiting for transfers between devices, body(): row_whole = lax.all_gather(absorbed, 'right', axis=0, tiled=True)  26.7 us
    dot_general x1, matrix products, body(): jnp.einsum('fkab,fkbc->fac', picked, edge_row, preferred_element_type=jnp...  9.24 us
    gather x1, local copies, waits for them, and re-layouts, body(): picked = jnp.take(gathered, local_index, axis=0)  6.73 us
    dot_general x1, matrix products, body(): jnp.einsum('gkab,gkbc->gac', edge_col, picked_col, preferred_element_type...  6.55 us
    gather x1, local copies, waits for them, and re-layouts, body(): picked_col = jnp.take(row_whole, source_col - row_base, axis=0)  5.81 us
  transfers between devices with their start and end apart: 4, of which 4 were waited for; matrix products, arithmetic and copies ran while one was open for 1% of the time, Pallas kernels for 0%

commit v1 on v0

v1 whole, which is shorter than its diff:
```python
import functools

import jax
import jax.numpy as jnp
from jax import lax
from jax.experimental import pallas as pl
from jax.experimental.pallas import tpu as pltpu
from jax.sharding import PartitionSpec as P

MESH = pl.DeviceIdType.MESH
PARTS = 2
LAG = 4


def wait_bytes(ref, sem):
    pltpu.make_async_copy(ref, ref, sem).wait()


def kernel(
    n_left, n_right,
    source_row, source_col, corner, edge_row, proj_row, edge_col, proj_col,
    absorbed_out, corner_out,
    gathered_0, gathered_1, edges_1, edges_2, projs_1, projs_2,
    own, prefix, suffix, to_right, to_left, row_sum, absorbed, col_part, col_in,
    edge_sem_1, edge_sem_2, proj_sem, local_sem,
    peer_send, peer_recv, pair_send, pair_recv,
    right_send, right_recv, left_send, left_recv, col_send, col_recv,
):
    held = corner.shape[0]
    size = corner.shape[1]
    half = size // PARTS
    sectors, entries_1 = source_row.shape
    groups, entries_2 = source_col.shape
    mine = absorbed_out.shape[0]
    chips = n_left // 2
    per_col = PARTS * sectors
    steps = PARTS * per_col
    depth = LAG * (n_right - 1)
    l, r = lax.axis_index("left"), lax.axis_index("right")
    core, chip = lax.rem(l, 2), lax.div(l, 2)
    gathered = (gathered_0, gathered_1)

    corner_copies = [
        pltpu.make_async_copy(
            corner.at[:, pl.ds(a * half, half), :], gathered[a].at[core, chip], local_sem.at[a])
        for a in range(PARTS)
    ]
    for copy in corner_copies:
        copy.start()

    @pl.loop(0, sectors)
    def _(f):
        pltpu.make_async_copy(edge_row.at[f], edges_1.at[f], edge_sem_1.at[f]).start()

    load_1 = pltpu.make_async_copy(proj_row, projs_1, proj_sem.at[0])
    load_1.start()

    @pl.loop(0, groups)
    def _(g):
        pltpu.make_async_copy(edge_col.at[g], edges_2.at[g], edge_sem_2.at[g]).start()

    load_2 = pltpu.make_async_copy(proj_col, projs_2, proj_sem.at[1])
    load_2.start()

    barrier = pltpu.get_barrier_semaphore()
    for off in range(1, n_left):
        pl.semaphore_signal(
            barrier, inc=1, device_id=(lax.rem(l + off, n_left), r), device_id_type=MESH)

    @pl.when(r > 0)
    def _():
        pl.semaphore_signal(barrier, inc=1, device_id=(l, r - 1), device_id_type=MESH)

    @pl.when(r < n_right - 1)
    def _():
        pl.semaphore_signal(barrier, inc=1, device_id=(l, r + 1), device_id_type=MESH)

    pl.semaphore_wait(
        barrier,
        n_left - 1 + jnp.where(r > 0, 1, 0) + jnp.where(r < n_right - 1, 1, 0))

    for a in range(PARTS):
        for off in range(1, chips):
            peer = lax.rem(chip + off, chips)
            pltpu.make_async_remote_copy(
                src_ref=corner.at[:, pl.ds(a * half, half), :],
                dst_ref=gathered[a].at[core, chip],
                send_sem=peer_send.at[a], recv_sem=peer_recv.at[a],
                device_id=(peer * 2 + core, r), device_id_type=MESH).start()

    def pair_copy(a):
        return pltpu.make_async_remote_copy(
            src_ref=gathered[a].at[core], dst_ref=gathered[a].at[core],
            send_sem=pair_send.at[a], recv_sem=pair_recv.at[a],
            device_id=(chip * 2 + 1 - core, r), device_id_type=MESH)

    def forward(a):
        corner_copies[a].wait()
        if chips > 1:
            wait_bytes(gathered[a].at[0, pl.ds(0, chips - 1)], peer_recv.at[a])
        pair_copy(a).start()

    @pl.when(r == 0)
    def _():
        prefix[...] = jnp.zeros_like(prefix)

    @pl.when(r == n_right - 1)
    def _():
        suffix[...] = jnp.zeros_like(suffix)

    def row_product(step, a):
        f = step - a * sectors
        if a == 0:
            wait_bytes(edges_1.at[f], edge_sem_1.at[f])
        total = None
        for k in range(entries_1):
            source = source_row[f, k]
            owner = lax.div(source, held * n_right)
            block = gathered[a][lax.rem(owner, 2), lax.div(owner, 2), lax.rem(source, held)]
            term = jnp.dot(block, edges_1[f, k], preferred_element_type=jnp.float32)
            total = term if total is None else total + term
        for c in range(PARTS):
            own[step + c * per_col] = total[:, c * half:(c + 1) * half]

    def travel(i):
        x = i - LAG * r

        @pl.when((x >= 0) & (x < steps))
        def _():
            @pl.when(r > 0)
            def _():
                wait_bytes(prefix.at[x], right_recv.at[x])

            @pl.when(r < n_right - 1)
            def _():
                to_right[x] = (prefix[x].astype(jnp.float32) + own[x]).astype(jnp.bfloat16)
                pltpu.make_async_remote_copy(
                    src_ref=to_right.at[x], dst_ref=prefix.at[x],
                    send_sem=right_send, recv_sem=right_recv.at[x],
                    device_id=(l, r + 1), device_id_type=MESH).start()

        y = i - LAG * (n_right - 1 - r)

        @pl.when((y >= 0) & (y < steps))
        def _():
            @pl.when(r < n_right - 1)
            def _():
                wait_bytes(suffix.at[y], left_recv.at[y])

            @pl.when(r > 0)
            def _():
                to_left[y] = (suffix[y].astype(jnp.float32) + own[y]).astype(jnp.bfloat16)
                pltpu.make_async_remote_copy(
                    src_ref=to_left.at[y], dst_ref=suffix.at[y],
                    send_sem=left_send, recv_sem=left_recv.at[y],
                    device_id=(l, r - 1), device_id_type=MESH).start()

        t = i - depth

        @pl.when((t >= 0) & (t < steps))
        def _():
            c, a, f = t // per_col, (t // sectors) % PARTS, t % sectors
            whole = prefix[t].astype(jnp.float32) + own[t] + suffix[t].astype(jnp.float32)
            row_sum[f, a] = whole.astype(jnp.bfloat16)

            @pl.when(a == PARTS - 1)
            def _():
                value = lax.dot_general(
                    projs_1[f], row_sum[f].reshape(size, half), (((0,), (0,)), ((), ())),
                    preferred_element_type=jnp.float32)
                absorbed[c, f] = value.astype(jnp.bfloat16)

    def column(c, g):
        if c == 0:
            wait_bytes(edges_2.at[g], edge_sem_2.at[g])
        total = None
        for k in range(entries_2):
            block = absorbed[c, lax.rem(source_col[g, k], sectors)]
            term = jnp.dot(edges_2[g, k], block, preferred_element_type=jnp.float32)
            total = term if total is None else total + term
        col_part[c, g] = total.astype(jnp.bfloat16).reshape(n_left, size // n_left, half)
        for off in range(1, n_left):
            there = lax.rem(l + off, n_left)
            pltpu.make_async_remote_copy(
                src_ref=col_part.at[c, g, there], dst_ref=col_in.at[c, g, l],
                send_sem=col_send, recv_sem=col_recv.at[c, g],
                device_id=(there, r), device_id_type=MESH).start()
        col_in[c, g, l] = col_part[c, g, l]

    forward(0)
    pair_copy(0).wait_recv()

    @pl.loop(0, sectors)
    def _(i):
        row_product(i, 0)
        travel(i)

        @pl.when(i == sectors // 2)
        def _():
            forward(1)

    pair_copy(1).wait_recv()

    load_1.wait()

    @pl.loop(sectors, per_col)
    def _(i):
        row_product(i, 1)
        travel(i)

    first = depth + per_col

    @pl.loop(per_col, steps + depth)
    def _(i):
        travel(i)

        @pl.when((i >= first) & (i < first + groups))
        def _():
            column(0, i - first)

    @pl.loop(0, groups)
    def _(g):
        column(1, g)

    for o in range(mine):
        for c in range(PARTS):
            absorbed_out[o, :, c * half:(c + 1) * half] = absorbed[c, r * mine + o]

    load_2.wait()

    @pl.loop(0, groups)
    def _(g):
        parts = []
        for c in range(PARTS):
            wait_bytes(col_in.at[c, g, pl.ds(0, n_left - 1)], col_recv.at[c, g])
            parts.append(jnp.sum(col_in[c, g].astype(jnp.float32), axis=0).astype(jnp.bfloat16))
        corner_out[g] = jnp.dot(
            jnp.concatenate(parts, axis=1), projs_2[g], preferred_element_type=jnp.float32
        ).astype(jnp.bfloat16)

    for a in range(PARTS):
        if chips > 1:
            wait_bytes(gathered[a].at[0, pl.ds(0, chips - 1)], peer_send.at[a])
        pair_copy(a).wait_send()

    @pl.when(r < n_right - 1)
    def _():
        wait_bytes(to_right, right_send)

    @pl.when(r > 0)
    def _():
        wait_bytes(to_left, left_send)

    wait_bytes(col_part.at[:, :, pl.ds(0, n_left - 1)], col_send)


def body(n_left, n_right, corner, edge_row, source_row, proj_row, edge_col, source_col, proj_col):
    held, size, _ = corner.shape
    sectors, entries_1 = source_row.shape
    groups, entries_2 = source_col.shape
    half = size // PARTS
    chips = n_left // 2
    steps = PARTS * PARTS * sectors
    rows = size // n_left
    bf16 = jnp.bfloat16
    dma = pltpu.SemaphoreType.DMA
    vmem = pl.BlockSpec(memory_space=pltpu.VMEM)
    smem = pl.BlockSpec(memory_space=pltpu.SMEM)
    far = pl.BlockSpec(memory_space=pl.ANY)
    gathered = pltpu.VMEM((2, chips, held, half, size), bf16)
    pieces = pltpu.VMEM((steps, half, half), bf16)
    columns = pltpu.VMEM((PARTS, groups, n_left, rows, half), bf16)
    return pl.pallas_call(
        functools.partial(kernel, n_left, n_right),
        out_shape=(
            jax.ShapeDtypeStruct((sectors // n_right, size, size), bf16),
            jax.ShapeDtypeStruct((groups, rows, size), bf16),
        ),
        in_specs=[smem, smem, far, far, far, far, far],
        out_specs=(vmem, vmem),
        scratch_shapes=[
            gathered, gathered,
            pltpu.VMEM(edge_row.shape, bf16), pltpu.VMEM(edge_col.shape, bf16),
            pltpu.VMEM(proj_row.shape, bf16), pltpu.VMEM(proj_col.shape, bf16),
            pltpu.VMEM((steps, half, half), jnp.float32),
            pieces, pieces, pieces, pieces,
            pltpu.VMEM((sectors, PARTS, half, half), bf16),
            pltpu.VMEM((PARTS, sectors, size, half), bf16),
            columns, columns,
            dma((sectors,)), dma((groups,)), dma((2,)), dma((PARTS,)),
            dma((PARTS,)), dma((PARTS,)), dma((PARTS,)), dma((PARTS,)),
            dma, dma((steps,)), dma, dma((steps,)), dma, dma((PARTS, groups)),
        ],
        compiler_params=pltpu.CompilerParams(
            collective_id=0, has_side_effects=True, vmem_limit_bytes=58 * 2**20),
        cost_estimate=pl.CostEstimate(
            flops=2 * size**3 * (sectors * (entries_1 + 1) + groups * (entries_2 + 1)),
            bytes_accessed=2 * (edge_row.size + edge_col.size + proj_row.size + proj_col.size),
            transcendentals=0),
    )(source_row, source_col, corner, edge_row, proj_row, edge_col, proj_col)


def solution(mesh):
    in_specs = (
        P(("left", "right"), None, None),
        P("left", "right", None, None),
        P("left", "right"),
        P("left", None, None),
        P("right", "left", None, None),
        P("right", "left"),
        P("right", None, None),
    )
    out_specs = (P(("left", "right"), None, None), P("right", "left", None))
    return jax.shard_map(
        functools.partial(body, mesh.shape["left"], mesh.shape["right"]),
        mesh=mesh, in_specs=in_specs, out_specs=out_specs, check_vma=False)
```

time: 163 us -> 56.7 us (0.35)
  waiting for transfers between devices: 116 us -> 0 us
  Pallas kernels: 0 us -> 52.7 us
  matrix products: 19.4 us -> 0 us
  between operations: 13.8 us -> 0.64 us
  local copies, waits for them, and re-layouts: 12.7 us -> 3.14 us
    reduce_scatter x2 -> x0, waiting for transfers between devices: 61 us -> none  [the longest x1 33.7 us: body(): lax.psum_scatter(partial_col.astype(jnp.bfloat16), 'left', scatter_dimens...]
    all_gather x2 -> x0, waiting for transfers between devices: 54.1 us -> none  [the longest x1 27.4 us: body(): gathered = lax.all_gather(corner, 'left', axis=0, tiled=True)]
    pallas_call x0 -> x1, Pallas kernels: none -> 52.7 us  [body(): pl.pallas_call(functools.partial(kernel, n_left, n_right), out_shape=(jax...]
    dot_general x4 -> x0, matrix products: 19.4 us -> none  [the longest x1 9.24 us: body(): jnp.einsum('fkab,fkbc->fac', picked, edge_row, preferred_element_type=jnp...]
    gather x2 -> x0, local copies, waits for them, and re-layouts: 12.5 us -> none  [the longest x1 6.73 us: body(): picked = jnp.take(gathered, local_index, axis=0)]
    unnamed x6 -> x2, local copies, waits for them, and re-layouts: 0.02 us -> 3.14 us
  transfers between devices with their start and end apart: 4 -> 0, of which waited for: 4 -> 0; matrix products, arithmetic and copies ran while one was open for 1% -> 0% of each run, Pallas kernels for 0% -> 0%
where the time goes in v1:
time: 56.7 us; the launch traced here: 56.5 us
  Pallas kernels  52.7 us (93%)
  local copies, waits for them, and re-layouts  3.14 us (6%)
  between operations  0.64 us (1%)
    pallas_call x1, Pallas kernels, body(): pl.pallas_call(functools.partial(kernel, n_left, n_right), out_shape=(jax...  52.7 us
    unnamed x2, local copies, waits for them, and re-layouts  3.14 us

profile of v1, /device:TPU:0, one launch (start us, length us, event | category | flops | bytes accessed | tf_op | source)
XLA Modules:
  0.0 56.5 jit_solution(1662857508928829245)
XLA Ops:
  0.6 52.7 %shard_map.86 = (bf16[2,256,256]{2,1,0:T(8,128)(2,1)}, bf16[4,32,256]{2,1,0:T(8,128)(2,1)}) custom-call(s32[8,8]{1,0:T(8,128)} %source_row.1, s32[4,10]{1,0:T(4,128)} %source_col.1, bf16[1,256,256]{2,1,0:T(8,128)(2,1)} %corner.1, bf16[8,8,256,256]{3,2,1,0:T(8,128)(2,1)} %edge_row.1, bf16[8,256,256]{2,1,0:T(8,128)(2,1)} %proj_row.1, ...), custom_call_target="tpu_custom_call" | custom-call | flops 3892314112 | bytes 15204352 | tf_op jit(solution)/shard_map/pallas_call | solution.py:273
  53.4 1.7 %copy.11 = bf16[2,256,256]{2,1,0:T(8,128)(2,1)} copy(bf16[2,256,256]{2,1,0:T(8,128)(2,1)} %get-tuple-element.4) | data formatting | bytes 524288
  55.0 1.5 %copy.12 = bf16[4,32,256]{2,1,0:T(8,128)(2,1)} copy(bf16[4,32,256]{2,1,0:T(8,128)(2,1)} %get-tuple-element.5) | data formatting | bytes 131072

commit v2 on v1

--- a/solution.py
+++ b/solution.py
@@ -9,7 +9,8 @@
 
 MESH = pl.DeviceIdType.MESH
 PARTS = 2
-LAG = 4
+LAGS = (2, 4)
+SLICES = 2
 
 
 def wait_bytes(ref, sem):
@@ -21,7 +22,7 @@
     source_row, source_col, corner, edge_row, proj_row, edge_col, proj_col,
     absorbed_out, corner_out,
     gathered_0, gathered_1, edges_1, edges_2, projs_1, projs_2,
-    own, prefix, suffix, to_right, to_left, row_sum, absorbed, col_part, col_in,
+    own, prefix, suffix, to_right, to_left, row_sum, absorbed, col_total, col_part, col_in,
     edge_sem_1, edge_sem_2, proj_sem, local_sem,
     peer_send, peer_recv, pair_send, pair_recv,
     right_send, right_recv, left_send, left_recv, col_send, col_recv,
@@ -35,7 +36,6 @@
     chips = n_left // 2
     per_col = PARTS * sectors
     steps = PARTS * per_col
-    depth = LAG * (n_right - 1)
     l, r = lax.axis_index("left"), lax.axis_index("right")
     core, chip = lax.rem(l, 2), lax.div(l, 2)
     gathered = (gathered_0, gathered_1)
@@ -48,12 +48,12 @@
     for copy in corner_copies:
         copy.start()
 
+    load_1 = pltpu.make_async_copy(proj_row, projs_1, proj_sem.at[0])
+    load_1.start()
+
     @pl.loop(0, sectors)
     def _(f):
         pltpu.make_async_copy(edge_row.at[f], edges_1.at[f], edge_sem_1.at[f]).start()
-
-    load_1 = pltpu.make_async_copy(proj_row, projs_1, proj_sem.at[0])
-    load_1.start()
 
     @pl.loop(0, groups)
     def _(g):
@@ -122,10 +122,15 @@
         for c in range(PARTS):
             own[step + c * per_col] = total[:, c * half:(c + 1) * half]
 
+    def piece(i, hops):
+        early, late = i - LAGS[0] * hops, i - LAGS[1] * hops
+        valid = ((early >= 0) & (early < per_col)) | ((late >= per_col) & (late < steps))
+        return jnp.where(early < per_col, early, late), valid
+
     def travel(i):
-        x = i - LAG * r
-
-        @pl.when((x >= 0) & (x < steps))
+        x, valid_x = piece(i, r)
+
+        @pl.when(valid_x)
         def _():
             @pl.when(r > 0)
             def _():
@@ -139,9 +144,9 @@
                     send_sem=right_send, recv_sem=right_recv.at[x],
                     device_id=(l, r + 1), device_id_type=MESH).start()
 
-        y = i - LAG * (n_right - 1 - r)
-
-        @pl.when((y >= 0) & (y < steps))
+        y, valid_y = piece(i, n_right - 1 - r)
+
+        @pl.when(valid_y)
         def _():
             @pl.when(r < n_right - 1)
             def _():
@@ -155,9 +160,9 @@
                     send_sem=left_send, recv_sem=left_recv.at[y],
                     device_id=(l, r - 1), device_id_type=MESH).start()
 
-        t = i - depth
-
-        @pl.when((t >= 0) & (t < steps))
+        t, valid_t = piece(i, n_right - 1)
+
+        @pl.when(valid_t)
         def _():
             c, a, f = t // per_col, (t // sectors) % PARTS, t % sectors
             whole = prefix[t].astype(jnp.float32) + own[t] + suffix[t].astype(jnp.float32)
@@ -165,19 +170,20 @@
 
             @pl.when(a == PARTS - 1)
             def _():
-                value = lax.dot_general(
-                    projs_1[f], row_sum[f].reshape(size, half), (((0,), (0,)), ((), ())),
+                value = jnp.dot(
+                    projs_1[f], row_sum[f].reshape(size, half),
                     preferred_element_type=jnp.float32)
                 absorbed[c, f] = value.astype(jnp.bfloat16)
 
-    def column(c, g):
-        if c == 0:
-            wait_bytes(edges_2.at[g], edge_sem_2.at[g])
+    def column_sum(c, g, ks):
         total = None
-        for k in range(entries_2):
+        for k in ks:
             block = absorbed[c, lax.rem(source_col[g, k], sectors)]
             term = jnp.dot(edges_2[g, k], block, preferred_element_type=jnp.float32)
             total = term if total is None else total + term
+        return total
+
+    def column_send(c, g, total):
         col_part[c, g] = total.astype(jnp.bfloat16).reshape(n_left, size // n_left, half)
         for off in range(1, n_left):
             there = lax.rem(l + off, n_left)
@@ -187,6 +193,12 @@
                 device_id=(there, r), device_id_type=MESH).start()
         col_in[c, g, l] = col_part[c, g, l]
 
+    load_1.wait()
+
+    @pl.loop(0, sectors)
+    def _(f):
+        projs_1[f] = projs_1[f].T
+
     forward(0)
     pair_copy(0).wait_recv()
 
@@ -201,26 +213,36 @@
 
     pair_copy(1).wait_recv()
 
-    load_1.wait()
-
     @pl.loop(sectors, per_col)
     def _(i):
         row_product(i, 1)
         travel(i)
 
-    first = depth + per_col
-
-    @pl.loop(per_col, steps + depth)
+    first = per_col + LAGS[0] * (n_right - 1)
+    cuts = [entries_2 * n // SLICES for n in range(SLICES + 1)]
+
+    @pl.loop(per_col, steps + LAGS[1] * (n_right - 1))
     def _(i):
         travel(i)
-
-        @pl.when((i >= first) & (i < first + groups))
-        def _():
-            column(0, i - first)
+        turn = i - first
+
+        for n in range(SLICES):
+            @pl.when((turn >= 0) & (turn < SLICES * groups) & (turn % SLICES == n))
+            def _():
+                g = turn // SLICES
+                if n == 0:
+                    wait_bytes(edges_2.at[g], edge_sem_2.at[g])
+                total = column_sum(0, g, range(cuts[n], cuts[n + 1]))
+                if n > 0:
+                    total = total + col_total[...]
+                if n < SLICES - 1:
+                    col_total[...] = total
+                else:
+                    column_send(0, g, total)
 
     @pl.loop(0, groups)
     def _(g):
-        column(1, g)
+        column_send(1, g, column_sum(1, g, range(entries_2)))
 
     for o in range(mine):
         for c in range(PARTS):
@@ -252,6 +274,14 @@
         wait_bytes(to_left, left_send)
 
     wait_bytes(col_part.at[:, :, pl.ds(0, n_left - 1)], col_send)
+
+
+def hand_over(a, b, a_out, b_out, sem):
+    copies = [pltpu.make_async_copy(a, a_out, sem.at[0]), pltpu.make_async_copy(b, b_out, sem.at[1])]
+    for copy in copies:
+        copy.start()
+    for copy in copies:
+        copy.wait()
 
 
 def body(n_left, n_right, corner, edge_row, source_row, proj_row, edge_col, source_col, proj_col):
@@ -270,7 +300,7 @@
     gathered = pltpu.VMEM((2, chips, held, half, size), bf16)
     pieces = pltpu.VMEM((steps, half, half), bf16)
     columns = pltpu.VMEM((PARTS, groups, n_left, rows, half), bf16)
-    return pl.pallas_call(
+    found = pl.pallas_call(
         functools.partial(kernel, n_left, n_right),
         out_shape=(
             jax.ShapeDtypeStruct((sectors // n_right, size, size), bf16),
@@ -286,6 +316,7 @@
             pieces, pieces, pieces, pieces,
             pltpu.VMEM((sectors, PARTS, half, half), bf16),
             pltpu.VMEM((PARTS, sectors, size, half), bf16),
+            pltpu.VMEM((size, half), jnp.float32),
             columns, columns,
             dma((sectors,)), dma((groups,)), dma((2,)), dma((PARTS,)),
             dma((PARTS,)), dma((PARTS,)), dma((PARTS,)), dma((PARTS,)),
@@ -298,6 +329,16 @@
             bytes_accessed=2 * (edge_row.size + edge_col.size + proj_row.size + proj_col.size),
             transcendentals=0),
     )(source_row, source_col, corner, edge_row, proj_row, edge_col, proj_col)
+    return pl.pallas_call(
+        hand_over,
+        out_shape=tuple(jax.ShapeDtypeStruct(x.shape, x.dtype) for x in found),
+        in_specs=[far, far],
+        out_specs=(far, far),
+        scratch_shapes=[dma((2,))],
+        compiler_params=pltpu.CompilerParams(vmem_limit_bytes=58 * 2**20),
+        cost_estimate=pl.CostEstimate(
+            flops=0, bytes_accessed=4 * sum(x.size for x in found), transcendentals=0),
+    )(*found)
 
 
 def solution(mesh):

time: 56.7 us -> 76.2 us (1.34)
  Pallas kernels: 52.7 us -> 75.4 us
  local copies, waits for them, and re-layouts: 3.14 us -> 0 us
    pallas_call x1, Pallas kernels: 52.7 us -> 64.3 us  [body(): pl.pallas_call(functools.partial(kernel, n_left, n_right), out_shape=(jax...]
    pallas_call x0 -> x1, Pallas kernels: none -> 11 us  [body(): pl.pallas_call(hand_over, out_shape=tuple((jax.ShapeDtypeStruct(x.shape,...]
    unnamed x2 -> x0, local copies, waits for them, and re-layouts: 3.14 us -> none
where the time goes in v2:
time: 76.2 us; the launch traced here: 76 us
  Pallas kernels  75.4 us (99%)
    pallas_call x1, Pallas kernels, body(): pl.pallas_call(functools.partial(kernel, n_left, n_right), out_shape=(jax...  64.3 us
    pallas_call x1, Pallas kernels, body(): pl.pallas_call(hand_over, out_shape=tuple((jax.ShapeDtypeStruct(x.shape,...  11 us

profile of v2, /device:TPU:0, one launch (start us, length us, event | category | flops | bytes accessed | tf_op | source)
XLA Modules:
  0.0 76.0 jit_solution(6849652391823694417)
XLA Ops:
  0.6 64.3 %shard_map.86 = (bf16[2,256,256]{2,1,0:T(8,128)(2,1)}, bf16[4,32,256]{2,1,0:T(8,128)(2,1)}) custom-call(s32[8,8]{1,0:T(8,128)} %source_row.1, s32[4,10]{1,0:T(4,128)} %source_col.1, bf16[1,256,256]{2,1,0:T(8,128)(2,1)} %corner.1, bf16[8,8,256,256]{3,2,1,0:T(8,128)(2,1)} %edge_row.1, bf16[8,256,256]{2,1,0:T(8,128)(2,1)} %proj_row.1, ...), custom_call_target="tpu_custom_call" | custom-call | flops 3892314112 | bytes 15204352 | tf_op jit(solution)/shard_map/pallas_call | solution.py:303
  65.0 11.0 %shard_map.87 = (bf16[2,256,256]{2,1,0:T(8,128)(2,1)}, bf16[4,32,256]{2,1,0:T(8,128)(2,1)}) custom-call(bf16[2,256,256]{2,1,0:T(8,128)(2,1)} %get-tuple-element.4.a, bf16[4,32,256]{2,1,0:T(8,128)(2,1)} %get-tuple-element.5.b), custom_call_target="tpu_custom_call" | custom-call | bytes 655360 | tf_op jit(solution)/shard_map/pallas_call | solution.py:332

commit v3 on v2

--- a/solution.py
+++ b/solution.py
@@ -9,7 +9,7 @@
 
 MESH = pl.DeviceIdType.MESH
 PARTS = 2
-LAGS = (2, 4)
+LAGS = (4, 6)
 SLICES = 2
 
 
@@ -276,12 +276,18 @@
     wait_bytes(col_part.at[:, :, pl.ds(0, n_left - 1)], col_send)
 
 
-def hand_over(a, b, a_out, b_out, sem):
-    copies = [pltpu.make_async_copy(a, a_out, sem.at[0]), pltpu.make_async_copy(b, b_out, sem.at[1])]
-    for copy in copies:
-        copy.start()
-    for copy in copies:
-        copy.wait()
+def hand_over(a, b, a_out, b_out, a_held, b_held, sem):
+    loads = [
+        pltpu.make_async_copy(a, a_held, sem.at[0]), pltpu.make_async_copy(b, b_held, sem.at[1])]
+    stores = [
+        pltpu.make_async_copy(a_held, a_out, sem.at[2]), pltpu.make_async_copy(b_held, b_out, sem.at[3])]
+    for load in loads:
+        load.start()
+    for load, store in zip(loads, stores):
+        load.wait()
+        store.start()
+    for store in stores:
+        store.wait()
 
 
 def body(n_left, n_right, corner, edge_row, source_row, proj_row, edge_col, source_col, proj_col):
@@ -334,7 +340,7 @@
         out_shape=tuple(jax.ShapeDtypeStruct(x.shape, x.dtype) for x in found),
         in_specs=[far, far],
         out_specs=(far, far),
-        scratch_shapes=[dma((2,))],
+        scratch_shapes=[pltpu.VMEM(x.shape, x.dtype) for x in found] + [dma((4,))],
         compiler_params=pltpu.CompilerParams(vmem_limit_bytes=58 * 2**20),
         cost_estimate=pl.CostEstimate(
             flops=0, bytes_accessed=4 * sum(x.size for x in found), transcendentals=0),

time: 76.2 us -> 54.8 us (0.72)
  Pallas kernels: 75.4 us -> 54 us
    pallas_call x1, Pallas kernels: 64.3 us -> 52.3 us  [body(): pl.pallas_call(functools.partial(kernel, n_left, n_right), out_shape=(jax...]
    pallas_call x1, Pallas kernels: 11 us -> 1.7 us  [body(): pl.pallas_call(hand_over, out_shape=tuple((jax.ShapeDtypeStruct(x.shape,...]
where the time goes in v3:
time: 54.8 us; the launch traced here: 54.6 us
  Pallas kernels  54 us (99%)
  between operations  0.64 us (1%)
    pallas_call x1, Pallas kernels, body(): pl.pallas_call(functools.partial(kernel, n_left, n_right), out_shape=(jax...  52.3 us
    pallas_call x1, Pallas kernels, body(): pl.pallas_call(hand_over, out_shape=tuple((jax.ShapeDtypeStruct(x.shape,...  1.7 us

profile of v3, /device:TPU:0, one launch (start us, length us, event | category | flops | bytes accessed | tf_op | source)
XLA Modules:
  0.0 54.6 jit_solution(14786026957423338117)
XLA Ops:
  0.6 52.3 %shard_map.86 = (bf16[2,256,256]{2,1,0:T(8,128)(2,1)}, bf16[4,32,256]{2,1,0:T(8,128)(2,1)}) custom-call(s32[8,8]{1,0:T(8,128)} %source_row.1, s32[4,10]{1,0:T(4,128)} %source_col.1, bf16[1,256,256]{2,1,0:T(8,128)(2,1)} %corner.1, bf16[8,8,256,256]{3,2,1,0:T(8,128)(2,1)} %edge_row.1, bf16[8,256,256]{2,1,0:T(8,128)(2,1)} %proj_row.1, ...), custom_call_target="tpu_custom_call" | custom-call | flops 3892314112 | bytes 15204352 | tf_op jit(solution)/shard_map/pallas_call | solution.py:309
  52.9 1.7 %shard_map.87 = (bf16[2,256,256]{2,1,0:T(8,128)(2,1)}, bf16[4,32,256]{2,1,0:T(8,128)(2,1)}) custom-call(bf16[2,256,256]{2,1,0:T(8,128)(2,1)} %get-tuple-element.4.a, bf16[4,32,256]{2,1,0:T(8,128)(2,1)} %get-tuple-element.5.b), custom_call_target="tpu_custom_call" | custom-call | bytes 655360 | tf_op jit(solution)/shard_map/pallas_call | solution.py:338

commit v4 on v3

--- a/solution.py
+++ b/solution.py
@@ -51,16 +51,11 @@
     load_1 = pltpu.make_async_copy(proj_row, projs_1, proj_sem.at[0])
     load_1.start()
 
-    @pl.loop(0, sectors)
-    def _(f):
+    def load_edges(f):
         pltpu.make_async_copy(edge_row.at[f], edges_1.at[f], edge_sem_1.at[f]).start()
 
-    @pl.loop(0, groups)
-    def _(g):
-        pltpu.make_async_copy(edge_col.at[g], edges_2.at[g], edge_sem_2.at[g]).start()
-
-    load_2 = pltpu.make_async_copy(proj_col, projs_2, proj_sem.at[1])
-    load_2.start()
+    for f in range(2):
+        load_edges(f)
 
     barrier = pltpu.get_barrier_semaphore()
     for off in range(1, n_left):
@@ -79,7 +74,7 @@
         barrier,
         n_left - 1 + jnp.where(r > 0, 1, 0) + jnp.where(r < n_right - 1, 1, 0))
 
-    for a in range(PARTS):
+    def gather(a):
         for off in range(1, chips):
             peer = lax.rem(chip + off, chips)
             pltpu.make_async_remote_copy(
@@ -99,6 +94,12 @@
         if chips > 1:
             wait_bytes(gathered[a].at[0, pl.ds(0, chips - 1)], peer_recv.at[a])
         pair_copy(a).start()
+
+    gather(0)
+
+    @pl.loop(2, sectors)
+    def _(f):
+        load_edges(f)
 
     @pl.when(r == 0)
     def _():
@@ -200,14 +201,22 @@
         projs_1[f] = projs_1[f].T
 
     forward(0)
+    gather(1)
     pair_copy(0).wait_recv()
+
+    @pl.loop(0, groups)
+    def _(g):
+        pltpu.make_async_copy(edge_col.at[g], edges_2.at[g], edge_sem_2.at[g]).start()
+
+    load_2 = pltpu.make_async_copy(proj_col, projs_2, proj_sem.at[1])
+    load_2.start()
 
     @pl.loop(0, sectors)
     def _(i):
         row_product(i, 0)
         travel(i)
 
-        @pl.when(i == sectors // 2)
+        @pl.when(i == sectors * 3 // 4)
         def _():
             forward(1)
 

time: 54.8 us -> 54.8 us (level)
  no operation moved by 1% of the time
where the time goes in v4:
time: 54.8 us; the launch traced here: 54.6 us
  Pallas kernels  53.9 us (98%)
  between operations  0.64 us (1%)
    pallas_call x1, Pallas kernels, body(): pl.pallas_call(functools.partial(kernel, n_left, n_right), out_shape=(jax...  52.2 us
    pallas_call x1, Pallas kernels, body(): pl.pallas_call(hand_over, out_shape=tuple((jax.ShapeDtypeStruct(x.shape,...  1.7 us

profile of v4, /device:TPU:0, one launch (start us, length us, event | category | flops | bytes accessed | tf_op | source)
XLA Modules:
  0.0 54.6 jit_solution(2973285385818166254)
XLA Ops:
  0.6 52.2 %shard_map.86 = (bf16[2,256,256]{2,1,0:T(8,128)(2,1)}, bf16[4,32,256]{2,1,0:T(8,128)(2,1)}) custom-call(s32[8,8]{1,0:T(8,128)} %source_row.1, s32[4,10]{1,0:T(4,128)} %source_col.1, bf16[1,256,256]{2,1,0:T(8,128)(2,1)} %corner.1, bf16[8,8,256,256]{3,2,1,0:T(8,128)(2,1)} %edge_row.1, bf16[8,256,256]{2,1,0:T(8,128)(2,1)} %proj_row.1, ...), custom_call_target="tpu_custom_call" | custom-call | flops 3892314112 | bytes 15204352 | tf_op jit(solution)/shard_map/pallas_call | solution.py:318
  52.9 1.7 %shard_map.87 = (bf16[2,256,256]{2,1,0:T(8,128)(2,1)}, bf16[4,32,256]{2,1,0:T(8,128)(2,1)}) custom-call(bf16[2,256,256]{2,1,0:T(8,128)(2,1)} %get-tuple-element.4.a, bf16[4,32,256]{2,1,0:T(8,128)(2,1)} %get-tuple-element.5.b), custom_call_target="tpu_custom_call" | custom-call | bytes 655360 | tf_op jit(solution)/shard_map/pallas_call | solution.py:347

commit v5 on v4

--- a/solution.py
+++ b/solution.py
@@ -9,7 +9,7 @@
 
 MESH = pl.DeviceIdType.MESH
 PARTS = 2
-LAGS = (4, 6)
+LAGS = (6, 8)
 SLICES = 2
 
 

time: 54.8 us -> 54.8 us (level)
  no operation moved by 1% of the time
where the time goes in v5:
time: 54.8 us; the launch traced here: 54.6 us
  Pallas kernels  53.9 us (98%)
  between operations  0.64 us (1%)
    pallas_call x1, Pallas kernels, body(): pl.pallas_call(functools.partial(kernel, n_left, n_right), out_shape=(jax...  52.2 us
    pallas_call x1, Pallas kernels, body(): pl.pallas_call(hand_over, out_shape=tuple((jax.ShapeDtypeStruct(x.shape,...  1.7 us

profile of v5, /device:TPU:0, one launch (start us, length us, event | category | flops | bytes accessed | tf_op | source)
XLA Modules:
  0.0 54.6 jit_solution(15255571447874683945)
XLA Ops:
  0.6 52.2 %shard_map.86 = (bf16[2,256,256]{2,1,0:T(8,128)(2,1)}, bf16[4,32,256]{2,1,0:T(8,128)(2,1)}) custom-call(s32[8,8]{1,0:T(8,128)} %source_row.1, s32[4,10]{1,0:T(4,128)} %source_col.1, bf16[1,256,256]{2,1,0:T(8,128)(2,1)} %corner.1, bf16[8,8,256,256]{3,2,1,0:T(8,128)(2,1)} %edge_row.1, bf16[8,256,256]{2,1,0:T(8,128)(2,1)} %proj_row.1, ...), custom_call_target="tpu_custom_call" | custom-call | flops 3892314112 | bytes 15204352 | tf_op jit(solution)/shard_map/pallas_call | solution.py:318
  52.9 1.7 %shard_map.87 = (bf16[2,256,256]{2,1,0:T(8,128)(2,1)}, bf16[4,32,256]{2,1,0:T(8,128)(2,1)}) custom-call(bf16[2,256,256]{2,1,0:T(8,128)(2,1)} %get-tuple-element.4.a, bf16[4,32,256]{2,1,0:T(8,128)(2,1)} %get-tuple-element.5.b), custom_call_target="tpu_custom_call" | custom-call | bytes 655360 | tf_op jit(solution)/shard_map/pallas_call | solution.py:347
